TPU v7x, 32 devices: a whole 2x2x4 slice. The times are simulated.
32 devices in a mesh: sec: 8 (over z, x), fld: 4 (over y, core).
Axes of the slice: x: 2, y: 2, z: 4, core: 2. Of those that a mesh axis runs over, the one named last changes fastest.
Arguments:
- surface: float32 [4, 256, 512], P('fld', 'sec'), may hold values from -6 to 6
- diffusivity: float32 [4, 256, 512], P('fld', 'sec'), may hold values from 0.02 to 0.24
- send_list: int32 [8, 8, 171], P('sec'), may hold values from 0 to 127
- recv_slot: int32 [1024, 4], P('sec'), may hold values from 0 to 1367, as said below
- weights: bfloat16 [1024, 4, 128, 128], P(('sec', 'fld')), may hold values from -0.25 to 0.25
Outputs:
- stepped: float32 [4, 256, 512], P('fld', 'sec')
- remapped: float32 [4, 256, 512], P('fld', 'sec')
Inputs may be any that keep to these rules, and one draw needn't show every extreme that they name: `recv_slot`: the 512 entries of one device's target blocks are distinct slots, all of devices of the other component; from one source device to one target device at most 171 slots are used, and that many in some pair.
All inputs are finite; a program needn't handle non-finite values.
Results may differ from a plain program's by a relative error of at most 0.0029.
Values may be sent and summed in bfloat16 or wider, within the bound.
A program may use at most 64 MiB of HBM per device.

v0:
```python
import jax
import jax.numpy as jnp
from jax import lax
from jax.sharding import PartitionSpec as P

SUBSTEPS = 4


def padded(block, sides, width):
    for axis, dim in sides:
        count = lax.axis_size(axis)
        forward = [(i, i + 1) for i in range(count - 1)]
        backward = [(target, source) for source, target in forward]
        low = lax.ppermute(
            lax.slice_in_dim(block, block.shape[dim] - width, None, axis=dim), axis, forward
        )
        high = lax.ppermute(lax.slice_in_dim(block, 0, width, axis=dim), axis, backward)
        block = jnp.concatenate([low, block, high], axis=dim)
    return block


def valid_rows(count, first, lowest, highest):
    global_row = first + jnp.arange(count, dtype=jnp.int32)
    return ((global_row >= lowest) & (global_row < highest))[None, :, None]


def update(extended, kappa):
    upper = extended[:, :-2]
    lower = extended[:, 2:]
    middle = extended[:, 1:-1]
    lap = upper + lower + jnp.roll(middle, 1, 2) + jnp.roll(middle, -1, 2) - 4.0 * middle
    return middle + kappa * lap


def per_device(surface, diffusivity, send_list, recv_slot, weights):
    sec_count = lax.axis_size("sec")
    here = lax.axis_index("sec")
    rows = surface.shape[1]
    cols = surface.shape[2]
    atmos_count = sec_count * 3 // 8
    is_ocean = here >= atmos_count
    lowest = jnp.where(is_ocean, atmos_count * rows, 0)
    highest = jnp.where(is_ocean, sec_count * rows, atmos_count * rows)
    field = surface
    for step in range(SUBSTEPS):
        extended = padded(field, (("sec", 1),), 1)
        inside = valid_rows(rows + 2, here * rows - 1, lowest, highest)
        extended = jnp.where(inside, extended, 0.0)
        field = update(extended, diffusivity)
    blocks = field.reshape(-1, 128).astype(jnp.bfloat16)
    outgoing = blocks[send_list[0]]
    incoming = lax.all_to_all(outgoing, "sec", split_axis=0, concat_axis=0, tiled=True)
    flat = incoming.reshape(-1, 128)
    pairs = flat[recv_slot]
    gathered = lax.all_to_all(pairs[None], "fld", split_axis=1, concat_axis=0, tiled=True)
    result = jnp.einsum("tkij,ftkj->fti", weights, gathered, preferred_element_type=jnp.float32)
    returned = lax.all_to_all(result, "fld", split_axis=0, concat_axis=1, tiled=True)
    remapped = returned.reshape(1, rows, cols)
    return (field, remapped)


def solution(mesh):
    return jax.shard_map(
        per_device,
        mesh=mesh,
        in_specs=(
            P("fld", "sec", None),
            P("fld", "sec", None),
            P("sec", None, None),
            P("sec", None),
            P(("sec", "fld"), None, None, None),
        ),
        out_specs=(P("fld", "sec", None), P("fld", "sec", None)),
        check_vma=False,
    )
```

profile of v0, /device:TPU:0, one launch (start us, length us, event | category | flops | bytes accessed | tf_op | source)
XLA Modules:
  0.0 82.4 jit_solution(17160284931847837862)
XLA Ops:
  0.6 0.7 fusion.34
  1.4 1.3 %collective-permute-start.1 = (f32[1,1,512]{2,1,0:T(1,128)S(1)}, f32[1,1,512]{2,1,0:T(1,128)S(1)}, u32[]{:S(2)}, u32[]{:S(2)}) collective-permute-start(f32[1,1,512]{2,1,0:T(1,128)S(1)} %get-tuple-element.27), channel_id=1, source_target_pairs={{4,0},{8,4},{12,8},{16,12},{20,16},{24,20},{28,24},{5,1},{9,5},{13... | collective-permute-start | bytes 6152 | tf_op jit(solution)/shard_map/ppermute | solution.py:17
  2.7 5.5 %collective-permute-start = (f32[1,1,512]{2,1,0:T(1,128)S(1)}, f32[1,1,512]{2,1,0:T(1,128)S(1)}, u32[]{:S(2)}, u32[]{:S(2)}) collective-permute-start(f32[1,1,512]{2,1,0:T(1,128)S(1)} %get-tuple-element.26), channel_id=1, source_target_pairs={{0,4},{4,8},{8,12},{12,16},{16,20},{20,24},{24,28},{1,5},{5,9},{9,... | collective-permute-start | bytes 6152 | tf_op jit(solution)/shard_map/ppermute | solution.py:14
  8.2 0.0 collective-permute-done.1
  8.2 1.3 %collective-permute-done = f32[1,1,512]{2,1,0:T(1,128)S(1)} collective-permute-done((f32[1,1,512]{2,1,0:T(1,128)S(1)}, f32[1,1,512]{2,1,0:T(1,128)S(1)}, u32[]{:S(2)}, u32[]{:S(2)}) %collective-permute-start) | collective-permute-done | bytes 2080 | tf_op jit(solution)/shard_map/ppermute | solution.py:14
  9.4 0.9 %maximum_select_fusion = f32[1,34,512]{2,1,0:T(8,128)S(1)} fusion(f32[1,1,512]{2,1,0:T(1,128)S(1)} %collective-permute-done.1, f32[1,32,512]{2,1,0:T(8,128)} %param.5, f32[1,1,512]{2,1,0:T(1,128)S(1)} %collective-permute-done, pred[34]{0:T(512)(128)(4,1)S(1)} %compare_and_fusion), kind=kLoop, calls=%fused_computation.4 | loop fusion | flops 52224 | bytes 139298 | tf_op jit(solution)/shard_map/jit(_where)/select_n | solution.py:48
  10.3 0.1 fusion.29
  10.4 0.0 copy-start
  10.4 0.1 fusion.30
  10.5 0.9 %fusion.20 = f32[1,32,512]{2,1,0:T(8,128)S(1)} fusion(f32[1,32,512]{2,1,0:T(8,128)} %param.6, f32[1,34,512]{2,1,0:T(8,128)S(1)} %maximum_select_fusion, f32[1,32,511]{2,1,0:T(8,128)S(1)} %get-tuple-element.17, f32[1,32,1]{2,1,0:T(8,128)S(1)} %get-tuple-element.19, f32[1,32,1]{2,1,0:T(8,128)S(1)} %get-tuple-element.18, f32[1,32,511]{2,1,0:T(8,128)S(1)} %get-tuple-element.16), kind=kLoop, calls=%fused_computation.31 | loop fusion | flops 147456 | bytes 458752 | tf_op jit(solution)/shard_map/add | solution.py:32
  11.5 1.3 %collective-permute-start.3 = (f32[1,1,512]{2,1,0:T(1,128)S(1)}, f32[1,1,512]{2,1,0:T(1,128)S(1)}, u32[]{:S(2)}, u32[]{:S(2)}) collective-permute-start(f32[1,1,512]{2,1,0:T(1,128)S(1)} %get-tuple-element.25), channel_id=1, source_target_pairs={{4,0},{8,4},{12,8},{16,12},{20,16},{24,20},{28,24},{5,1},{9,5},{13... | collective-permute-start | bytes 6152 | tf_op jit(solution)/shard_map/ppermute | solution.py:17
  12.8 5.4 %collective-permute-start.2 = (f32[1,1,512]{2,1,0:T(1,128)S(1)}, f32[1,1,512]{2,1,0:T(1,128)S(1)}, u32[]{:S(2)}, u32[]{:S(2)}) collective-permute-start(f32[1,1,512]{2,1,0:T(1,128)S(1)} %get-tuple-element.24), channel_id=1, source_target_pairs={{0,4},{4,8},{8,12},{12,16},{16,20},{20,24},{24,28},{1,5},{5,9},{9,... | collective-permute-start | bytes 6152 | tf_op jit(solution)/shard_map/ppermute | solution.py:14
  18.2 0.0 collective-permute-done.3
  18.2 1.3 %collective-permute-done.2 = f32[1,1,512]{2,1,0:T(1,128)S(1)} collective-permute-done((f32[1,1,512]{2,1,0:T(1,128)S(1)}, f32[1,1,512]{2,1,0:T(1,128)S(1)}, u32[]{:S(2)}, u32[]{:S(2)}) %collective-permute-start.2) | collective-permute-done | bytes 2080 | tf_op jit(solution)/shard_map/ppermute | solution.py:14
  19.5 0.1 maximum_select_fusion.1
  19.6 0.1 fusion.27
  19.7 0.1 fusion.28
  19.8 0.9 %fusion.15 = f32[1,32,512]{2,1,0:T(8,128)S(1)} fusion(f32[1,32,512]{2,1,0:T(8,128)} %param.6, f32[1,34,512]{2,1,0:T(8,128)S(1)} %maximum_select_fusion.1, f32[1,32,511]{2,1,0:T(8,128)S(1)} %get-tuple-element.13, f32[1,32,1]{2,1,0:T(8,128)S(1)} %get-tuple-element.15, f32[1,32,1]{2,1,0:T(8,128)S(1)} %get-tuple-element.14, f32[1,32,511]{2,1,0:T(8,128)S(1)} %get-tuple-element.12), kind=kLoop, calls=%fused_computation.25 | loop fusion | flops 147456 | bytes 458752 | tf_op jit(solution)/shard_map/add | solution.py:32
  20.7 1.3 %collective-permute-start.5 = (f32[1,1,512]{2,1,0:T(1,128)S(1)}, f32[1,1,512]{2,1,0:T(1,128)S(1)}, u32[]{:S(2)}, u32[]{:S(2)}) collective-permute-start(f32[1,1,512]{2,1,0:T(1,128)S(1)} %get-tuple-element.23), channel_id=1, source_target_pairs={{4,0},{8,4},{12,8},{16,12},{20,16},{24,20},{28,24},{5,1},{9,5},{13... | collective-permute-start | bytes 6152 | tf_op jit(solution)/shard_map/ppermute | solution.py:17
  22.0 5.7 %collective-permute-start.4 = (f32[1,1,512]{2,1,0:T(1,128)S(1)}, f32[1,1,512]{2,1,0:T(1,128)S(1)}, u32[]{:S(2)}, u32[]{:S(2)}) collective-permute-start(f32[1,1,512]{2,1,0:T(1,128)S(1)} %get-tuple-element.22), channel_id=1, source_target_pairs={{0,4},{4,8},{8,12},{12,16},{16,20},{20,24},{24,28},{1,5},{5,9},{9,... | collective-permute-start | bytes 6152 | tf_op jit(solution)/shard_map/ppermute | solution.py:14
  27.7 0.7 compare_select_fusion
  28.4 0.1 reshape.296
  28.5 0.0 collective-permute-done.5
  28.5 0.5 collective-permute-done.4
  29.0 0.1 maximum_select_fusion.2
  29.1 0.1 fusion.25
  29.2 0.1 fusion.26
  29.3 0.9 %fusion.10 = f32[1,32,512]{2,1,0:T(8,128)S(1)} fusion(f32[1,32,512]{2,1,0:T(8,128)} %param.6, f32[1,34,512]{2,1,0:T(8,128)S(1)} %maximum_select_fusion.2, f32[1,32,511]{2,1,0:T(8,128)S(1)} %get-tuple-element.9, f32[1,32,1]{2,1,0:T(8,128)S(1)} %get-tuple-element.11, f32[1,32,1]{2,1,0:T(8,128)S(1)} %get-tuple-element.10, f32[1,32,511]{2,1,0:T(8,128)S(1)} %get-tuple-element.8), kind=kLoop, calls=%fused_computation.19 | loop fusion | flops 147456 | bytes 458752 | tf_op jit(solution)/shard_map/add | solution.py:32
  30.2 1.3 %collective-permute-start.7 = (f32[1,1,512]{2,1,0:T(1,128)S(1)}, f32[1,1,512]{2,1,0:T(1,128)S(1)}, u32[]{:S(2)}, u32[]{:S(2)}) collective-permute-start(f32[1,1,512]{2,1,0:T(1,128)S(1)} %get-tuple-element.21), channel_id=1, source_target_pairs={{4,0},{8,4},{12,8},{16,12},{20,16},{24,20},{28,24},{5,1},{9,5},{13... | collective-permute-start | bytes 6152 | tf_op jit(solution)/shard_map/ppermute | solution.py:17
  31.5 5.7 %collective-permute-start.6 = (f32[1,1,512]{2,1,0:T(1,128)S(1)}, f32[1,1,512]{2,1,0:T(1,128)S(1)}, u32[]{:S(2)}, u32[]{:S(2)}) collective-permute-start(f32[1,1,512]{2,1,0:T(1,128)S(1)} %get-tuple-element.20), channel_id=1, source_target_pairs={{0,4},{4,8},{8,12},{12,16},{16,20},{20,24},{24,28},{1,5},{5,9},{9,... | collective-permute-start | bytes 6152 | tf_op jit(solution)/shard_map/ppermute | solution.py:14
  37.2 0.0 collective-permute-done.7
  37.3 1.3 %collective-permute-done.6 = f32[1,1,512]{2,1,0:T(1,128)S(1)} collective-permute-done((f32[1,1,512]{2,1,0:T(1,128)S(1)}, f32[1,1,512]{2,1,0:T(1,128)S(1)}, u32[]{:S(2)}, u32[]{:S(2)}) %collective-permute-start.6) | collective-permute-done | bytes 2080 | tf_op jit(solution)/shard_map/ppermute | solution.py:14
  38.5 0.1 maximum_select_fusion.3
  38.6 0.1 fusion.23
  38.7 0.1 fusion.24
  38.8 1.6 %fusion.21 = (bf16[1,32,512]{2,1,0:T(8,128)(2,1)S(1)}, f32[1,32,512]{2,1,0:T(8,128)}) fusion(f32[1,32,512]{2,1,0:T(8,128)} %param.6, f32[1,32,1]{2,1,0:T(8,128)S(1)} %get-tuple-element.5, f32[1,32,511]{2,1,0:T(8,128)S(1)} %get-tuple-element.7, f32[1,32,511]{2,1,0:T(8,128)S(1)} %get-tuple-element.6, f32[1,32,1]{2,1,0:T(8,128)S(1)} %get-tuple-element.4, ...), kind=kLoop, calls=%fused_computation.37 | loop fusion | flops 163840 | bytes 491520 | tf_op jit(solution)/shard_map/convert_element_type | solution.py:50
  40.4 3.3 %gather_fusion = bf16[1368,128]{1,0:T(8,128)(2,1)S(1)} fusion(bf16[128,128]{1,0:T(8,128)(2,1)S(1)} %convert_element_type.7, s32[2048]{0:T(1024)S(1)} %pad_clamp_fusion), kind=kCustom, calls=%fused_computation | custom fusion | bytes 705888 | tf_op jit(solution)/shard_map/gather | solution.py:51
  43.7 0.8 %reshape.295 = bf16[8,171,128]{2,1,0:T(8,128)(2,1)} reshape(bf16[1368,128]{1,0:T(8,128)(2,1)S(1)} %gather_fusion) | data formatting | bytes 700416 | tf_op jit(solution)/shard_map/gather | solution.py:51
  44.5 9.7 %all-to-all-start = ((bf16[8,171,128]{2,1,0:T(8,128)(2,1)}), bf16[8,171,128]{2,1,0:T(8,128)(2,1)S(1)}, u32[]{:S(2)}, u32[]{:S(2)}) async-start(bf16[8,171,128]{2,1,0:T(8,128)(2,1)} %reshape.295), calls=%async_computation | async-start | bytes 720896 | tf_op jit(solution)/shard_map/all_to_all | solution.py:52
  54.3 0.0 copy-done
  54.3 0.1 copy.11
  54.4 0.1 reshape.304
  54.5 8.7 %all-to-all-done = bf16[8,171,128]{2,1,0:T(8,128)(2,1)S(1)} async-done(((bf16[8,171,128]{2,1,0:T(8,128)(2,1)}), bf16[8,171,128]{2,1,0:T(8,128)(2,1)S(1)}, u32[]{:S(2)}, u32[]{:S(2)}) %all-to-all-start) | async-done | bytes 350240 | tf_op jit(solution)/shard_map/all_to_all | solution.py:52
  63.2 0.1 reshape.292
  63.3 1.3 %gather_fusion.1 = bf16[512,128]{1,0:T(8,128)(2,1)S(1)} fusion(bf16[1368,128]{1,0:T(8,128)(2,1)S(1)} %reshape.292, s32[1024]{0:T(1024)S(1)} %pad_clamp_fusion.1), kind=kCustom, calls=%fused_computation.1 | custom fusion | bytes 264192 | tf_op jit(solution)/shard_map/gather | solution.py:54
  64.7 7.2 %all_to_all.26 = bf16[1,128,4,128]{3,2,0,1:T(4,128)(2,1)S(1)} all-to-all(bf16[1,128,4,128]{3,2,0,1:T(4,128)(2,1)S(1)} %bitcast.14), channel_id=1, replica_groups=mesh['sec'=8,'fld'=4] {'fld'}, dimensions={1} | all-to-all | bytes 262144 | tf_op jit(solution)/shard_map/all_to_all | solution.py:55
  71.9 3.4 %convolution_bitcast_fusion = f32[4,32,128]{2,0,1:T(4,128)S(1)} fusion(bf16[32,4,128,128]{3,2,1,0:T(8,128)(2,1)} %param.9, bf16[4,32,4,128]{3,2,1,0:T(4,128)(2,1)S(1)} %bitcast.15), kind=kOutput, calls=%fused_computation.2 | convolution fusion | flops 16777216 | bytes 4390912 | tf_op jit(solution)/shard_map/tkij,ftkj->fti/dot_general | solution.py:56
  75.3 6.5 %all_to_all.27 = f32[4,32,128]{2,1,0:T(8,128)S(1)} all-to-all(f32[4,32,128]{2,1,0:T(8,128)S(1)} %copy.15), channel_id=1, replica_groups=mesh['sec'=8,'fld'=4] {'fld'}, dimensions={0} | all-to-all | bytes 131072 | tf_op jit(solution)/shard_map/all_to_all | solution.py:57
  81.8 0.6 reshape.293
  (9 shorter events, 0.1 us)
Async XLA Ops:
  1.4 6.8 %collective-permute-start.1 = (f32[1,1,512]{2,1,0:T(1,128)S(1)}, f32[1,1,512]{2,1,0:T(1,128)S(1)}, u32[]{:S(2)}, u32[]{:S(2)}) collective-permute-start(f32[1,1,512]{2,1,0:T(1,128)S(1)} %get-tuple-element.27), channel_id=1, source_target_pairs={{4,0},{8,4},{12,8},{16,12},{20,16},{24,20},{28,24},{5,1},{9,5},{13... | collective-permute-start | bytes 6152 | tf_op jit(solution)/shard_map/ppermute | solution.py:17
  2.7 6.8 %collective-permute-start = (f32[1,1,512]{2,1,0:T(1,128)S(1)}, f32[1,1,512]{2,1,0:T(1,128)S(1)}, u32[]{:S(2)}, u32[]{:S(2)}) collective-permute-start(f32[1,1,512]{2,1,0:T(1,128)S(1)} %get-tuple-element.26), channel_id=1, source_target_pairs={{0,4},{4,8},{8,12},{12,16},{16,20},{20,24},{24,28},{1,5},{5,9},{9,... | collective-permute-start | bytes 6152 | tf_op jit(solution)/shard_map/ppermute | solution.py:14
  10.4 43.8 %copy-start = (s32[128,4]{0,1:T(4,128)S(1)}, s32[128,4]{0,1:T(4,128)}, u32[]{:S(2)}) copy-start(s32[128,4]{0,1:T(4,128)} %param.8) | copy-start | bytes 6148
  11.5 6.8 %collective-permute-start.3 = (f32[1,1,512]{2,1,0:T(1,128)S(1)}, f32[1,1,512]{2,1,0:T(1,128)S(1)}, u32[]{:S(2)}, u32[]{:S(2)}) collective-permute-start(f32[1,1,512]{2,1,0:T(1,128)S(1)} %get-tuple-element.25), channel_id=1, source_target_pairs={{4,0},{8,4},{12,8},{16,12},{20,16},{24,20},{28,24},{5,1},{9,5},{13... | collective-permute-start | bytes 6152 | tf_op jit(solution)/shard_map/ppermute | solution.py:17
  12.8 6.7 %collective-permute-start.2 = (f32[1,1,512]{2,1,0:T(1,128)S(1)}, f32[1,1,512]{2,1,0:T(1,128)S(1)}, u32[]{:S(2)}, u32[]{:S(2)}) collective-permute-start(f32[1,1,512]{2,1,0:T(1,128)S(1)} %get-tuple-element.24), channel_id=1, source_target_pairs={{0,4},{4,8},{8,12},{12,16},{16,20},{20,24},{24,28},{1,5},{5,9},{9,... | collective-permute-start | bytes 6152 | tf_op jit(solution)/shard_map/ppermute | solution.py:14
  20.7 7.8 %collective-permute-start.5 = (f32[1,1,512]{2,1,0:T(1,128)S(1)}, f32[1,1,512]{2,1,0:T(1,128)S(1)}, u32[]{:S(2)}, u32[]{:S(2)}) collective-permute-start(f32[1,1,512]{2,1,0:T(1,128)S(1)} %get-tuple-element.23), channel_id=1, source_target_pairs={{4,0},{8,4},{12,8},{16,12},{20,16},{24,20},{28,24},{5,1},{9,5},{13... | collective-permute-start | bytes 6152 | tf_op jit(solution)/shard_map/ppermute | solution.py:17
  22.0 7.0 %collective-permute-start.4 = (f32[1,1,512]{2,1,0:T(1,128)S(1)}, f32[1,1,512]{2,1,0:T(1,128)S(1)}, u32[]{:S(2)}, u32[]{:S(2)}) collective-permute-start(f32[1,1,512]{2,1,0:T(1,128)S(1)} %get-tuple-element.22), channel_id=1, source_target_pairs={{0,4},{4,8},{8,12},{12,16},{16,20},{20,24},{24,28},{1,5},{5,9},{9,... | collective-permute-start | bytes 6152 | tf_op jit(solution)/shard_map/ppermute | solution.py:14
  30.2 7.0 %collective-permute-start.7 = (f32[1,1,512]{2,1,0:T(1,128)S(1)}, f32[1,1,512]{2,1,0:T(1,128)S(1)}, u32[]{:S(2)}, u32[]{:S(2)}) collective-permute-start(f32[1,1,512]{2,1,0:T(1,128)S(1)} %get-tuple-element.21), channel_id=1, source_target_pairs={{4,0},{8,4},{12,8},{16,12},{20,16},{24,20},{28,24},{5,1},{9,5},{13... | collective-permute-start | bytes 6152 | tf_op jit(solution)/shard_map/ppermute | solution.py:17
  31.5 7.0 %collective-permute-start.6 = (f32[1,1,512]{2,1,0:T(1,128)S(1)}, f32[1,1,512]{2,1,0:T(1,128)S(1)}, u32[]{:S(2)}, u32[]{:S(2)}) collective-permute-start(f32[1,1,512]{2,1,0:T(1,128)S(1)} %get-tuple-element.20), channel_id=1, source_target_pairs={{0,4},{4,8},{8,12},{12,16},{16,20},{20,24},{24,28},{1,5},{5,9},{9,... | collective-permute-start | bytes 6152 | tf_op jit(solution)/shard_map/ppermute | solution.py:14
  44.5 18.7 %all-to-all-start = ((bf16[8,171,128]{2,1,0:T(8,128)(2,1)}), bf16[8,171,128]{2,1,0:T(8,128)(2,1)S(1)}, u32[]{:S(2)}, u32[]{:S(2)}) async-start(bf16[8,171,128]{2,1,0:T(8,128)(2,1)} %reshape.295), calls=%async_computation | async-start | bytes 720896 | tf_op jit(solution)/shard_map/all_to_all | solution.py:52
where the time goes:
time: 83.2 us; the launch traced here: 82.4 us
  starting transfers between devices  37.2 us (45%)
  blocking collectives  13.7 us (16%)
  waiting for transfers between devices  13 us (16%)
  local copies, waits for them, and re-layouts  8 us (10%)
  other arithmetic  6.24 us (8%)
  matrix products  3.38 us (4%)
  between operations  0.88 us (1%)
    ppermute x4, starting transfers between devices, padded(): lax.ppermute(lax.slice_in_dim(block, block.shape[dim] - width, None, axis...  22.3 us
    all_to_all x1, starting transfers between devices, per_device(): lax.all_to_all(outgoing, 'sec', split_axis=0, concat_axis=0, tiled=True)  9.72 us
    all_to_all x1, waiting for transfers between devices, per_device(): lax.all_to_all(outgoing, 'sec', split_axis=0, concat_axis=0, tiled=True)  8.69 us
    all_to_all x1, blocking collectives, per_device(): lax.all_to_all(pairs[None], 'fld', split_axis=1, concat_axis=0, tiled=True)  7.22 us
    all_to_all x1, blocking collectives, per_device(): lax.all_to_all(result, 'fld', split_axis=0, concat_axis=1, tiled=True)  6.49 us
    ppermute x4, starting transfers between devices, padded(): lax.ppermute(lax.slice_in_dim(block, 0, width, axis=dim), axis, backward)  5.16 us
    ppermute x4, waiting for transfers between devices, padded(): lax.ppermute(lax.slice_in_dim(block, block.shape[dim] - width, None, axis...  4.29 us
    gather x2, local copies, waits for them, and re-layouts, per_device(): outgoing = blocks[send_list[0]]  4.17 us
  transfers between devices with their start and end apart: 9, of which 5 were waited for; matrix products, arithmetic and copies ran while one was open for 1% of the time, Pallas kernels for 0%

commit v1 on v0

--- a/solution.py
+++ b/solution.py
@@ -54,7 +54,15 @@
     pairs = flat[recv_slot]
     gathered = lax.all_to_all(pairs[None], "fld", split_axis=1, concat_axis=0, tiled=True)
     result = jnp.einsum("tkij,ftkj->fti", weights, gathered, preferred_element_type=jnp.float32)
-    returned = lax.all_to_all(result, "fld", split_axis=0, concat_axis=1, tiled=True)
+    ways, here_2 = (lax.axis_size("fld"), lax.axis_index("fld"))
+    width_2 = result.shape[0] // ways
+    turned = jnp.roll(result, -here_2 * width_2, axis=0)
+    got = [lax.slice_in_dim(turned, 0, width_2, axis=0)]
+    for far in range(1, ways):
+        sent = lax.slice_in_dim(turned, far * width_2, (far + 1) * width_2, axis=0)
+        got.append(lax.ppermute(sent, "fld", [(d, (d + far) % ways) for d in range(ways)]))
+    line = jnp.concatenate(got[::-1], axis=1)
+    returned = jnp.roll(line, (here_2 + 1) * got[0].shape[1], axis=1)
     remapped = returned.reshape(1, rows, cols)
     return (field, remapped)
 

time: 83.2 us -> 83 us (level)
  waiting for transfers between devices: 13 us -> 32.3 us
  blocking collectives: 13.7 us -> 0 us
  starting transfers between devices: 37.2 us -> 30.3 us
  local copies, waits for them, and re-layouts: 8 us -> 8.87 us
    ppermute x4, waiting for transfers between devices: 0.01 us -> 15.8 us  [padded(): lax.ppermute(lax.slice_in_dim(block, 0, width, axis=dim), axis, backward)]
    all_to_all x2 -> x0, blocking collectives: 13.7 us -> none  [the longest x1 7.22 us: per_device(): lax.all_to_all(pairs[None], 'fld', split_axis=1, concat_axis=0, tiled=True)]
    all_to_all x1, starting transfers between devices: 9.72 us -> 3.78 us  [per_device(): lax.all_to_all(outgoing, 'sec', split_axis=0, concat_axis=0, tiled=True)]
    ppermute x4, starting transfers between devices: 22.3 us -> 16.9 us  [padded(): lax.ppermute(lax.slice_in_dim(block, block.shape[dim] - width, None, axis...]
    all_to_all x0 -> x1, waiting for transfers between devices: none -> 4.57 us  [per_device(): lax.all_to_all(pairs[None], 'fld', split_axis=1, concat_axis=0, tiled=True)]
    ppermute x4, waiting for transfers between devices: 4.29 us -> 0.01 us  [padded(): lax.ppermute(lax.slice_in_dim(block, block.shape[dim] - width, None, axis...]
    all_to_all x0 -> x1, starting transfers between devices: none -> 3.32 us  [per_device(): lax.all_to_all(pairs[None], 'fld', split_axis=1, concat_axis=0, tiled=True)]
    ppermute x0 -> x3, waiting for transfers between devices: none -> 3.15 us  [per_device(): lax.ppermute(sent, 'fld', [(d, (d + far) % ways) for d in range(ways)])]
  transfers between devices with their start and end apart: 9 -> 13, of which waited for: 5 -> 9; matrix products, arithmetic and copies ran while one was open for 1% -> 1% of each run, Pallas kernels for 0% -> 0%
where the time goes in v1:
time: 83 us; the launch traced here: 82.1 us
  waiting for transfers between devices  32.3 us (39%)
  starting transfers between devices  30.3 us (37%)
  local copies, waits for them, and re-layouts  8.87 us (11%)
  other arithmetic  6.31 us (8%)
  matrix products  3.37 us (4%)
  between operations  0.97 us (1%)
    ppermute x4, starting transfers between devices, padded(): lax.ppermute(lax.slice_in_dim(block, block.shape[dim] - width, None, axis...  16.9 us
    ppermute x4, waiting for transfers between devices, padded(): lax.ppermute(lax.slice_in_dim(block, 0, width, axis=dim), axis, backward)  15.8 us
    all_to_all x1, waiting for transfers between devices, per_device(): lax.all_to_all(outgoing, 'sec', split_axis=0, concat_axis=0, tiled=True)  8.69 us
    ppermute x4, starting transfers between devices, padded(): lax.ppermute(lax.slice_in_dim(block, 0, width, axis=dim), axis, backward)  5.17 us
    all_to_all x1, waiting for transfers between devices, per_device(): lax.all_to_all(pairs[None], 'fld', split_axis=1, concat_axis=0, tiled=True)  4.57 us
    gather x2, local copies, waits for them, and re-layouts, per_device(): outgoing = blocks[send_list[0]]  4.16 us
    all_to_all x1, starting transfers between devices, per_device(): lax.all_to_all(outgoing, 'sec', split_axis=0, concat_axis=0, tiled=True)  3.78 us
    dot_general x1, matrix products, per_device(): jnp.einsum('tkij,ftkj->fti', weights, gathered, preferred_element_type=jn...  3.37 us
  transfers between devices with their start and end apart: 13, of which 9 were waited for; matrix products, arithmetic and copies ran while one was open for 1% of the time, Pallas kernels for 0%

profile of v1, /device:TPU:0, one launch (start us, length us, event | category | flops | bytes accessed | tf_op | source)
XLA Modules:
  0.0 82.1 jit_solution(6985509997546181005)
XLA Ops:
  0.6 0.7 fusion.36
  1.4 4.8 %collective-permute-start = (f32[1,1,512]{2,1,0:T(1,128)S(1)}, f32[1,1,512]{2,1,0:T(1,128)S(1)}, u32[]{:S(2)}, u32[]{:S(2)}) collective-permute-start(f32[1,1,512]{2,1,0:T(1,128)S(1)} %get-tuple-element.29), channel_id=1, source_target_pairs={{0,4},{4,8},{8,12},{12,16},{16,20},{20,24},{24,28},{1,5},{5,9},{9,... | collective-permute-start | bytes 6152 | tf_op jit(solution)/shard_map/ppermute | solution.py:14
  6.2 1.3 %collective-permute-start.1 = (f32[1,1,512]{2,1,0:T(1,128)S(1)}, f32[1,1,512]{2,1,0:T(1,128)S(1)}, u32[]{:S(2)}, u32[]{:S(2)}) collective-permute-start(f32[1,1,512]{2,1,0:T(1,128)S(1)} %get-tuple-element.30), channel_id=1, source_target_pairs={{4,0},{8,4},{12,8},{16,12},{20,16},{24,20},{28,24},{5,1},{9,5},{13... | collective-permute-start | bytes 6152 | tf_op jit(solution)/shard_map/ppermute | solution.py:17
  7.5 0.0 collective-permute-done
  7.5 4.1 %collective-permute-done.1 = f32[1,1,512]{2,1,0:T(1,128)S(1)} collective-permute-done((f32[1,1,512]{2,1,0:T(1,128)S(1)}, f32[1,1,512]{2,1,0:T(1,128)S(1)}, u32[]{:S(2)}, u32[]{:S(2)}) %collective-permute-start.1) | collective-permute-done | bytes 2080 | tf_op jit(solution)/shard_map/ppermute | solution.py:17
  11.7 0.9 %maximum_select_fusion = f32[1,34,512]{2,1,0:T(8,128)S(1)} fusion(f32[1,1,512]{2,1,0:T(1,128)S(1)} %collective-permute-done.1, f32[1,32,512]{2,1,0:T(8,128)} %param.5, f32[1,1,512]{2,1,0:T(1,128)S(1)} %collective-permute-done, pred[34]{0:T(512)(128)(4,1)S(1)} %compare_and_fusion), kind=kLoop, calls=%fused_computation.6 | loop fusion | flops 52224 | bytes 139298 | tf_op jit(solution)/shard_map/jit(_where)/select_n | solution.py:48
  12.6 0.1 fusion.30
  12.7 0.0 copy-start
  12.7 0.1 fusion.31
  12.8 0.9 %fusion.21 = f32[1,32,512]{2,1,0:T(8,128)S(1)} fusion(f32[1,32,512]{2,1,0:T(8,128)} %param.6, f32[1,34,512]{2,1,0:T(8,128)S(1)} %maximum_select_fusion, f32[1,32,511]{2,1,0:T(8,128)S(1)} %get-tuple-element.17, f32[1,32,1]{2,1,0:T(8,128)S(1)} %get-tuple-element.19, f32[1,32,1]{2,1,0:T(8,128)S(1)} %get-tuple-element.18, f32[1,32,511]{2,1,0:T(8,128)S(1)} %get-tuple-element.16), kind=kLoop, calls=%fused_computation.34 | loop fusion | flops 147456 | bytes 458752 | tf_op jit(solution)/shard_map/add | solution.py:32
  13.7 4.4 %collective-permute-start.2 = (f32[1,1,512]{2,1,0:T(1,128)S(1)}, f32[1,1,512]{2,1,0:T(1,128)S(1)}, u32[]{:S(2)}, u32[]{:S(2)}) collective-permute-start(f32[1,1,512]{2,1,0:T(1,128)S(1)} %get-tuple-element.27), channel_id=1, source_target_pairs={{0,4},{4,8},{8,12},{12,16},{16,20},{20,24},{24,28},{1,5},{5,9},{9,... | collective-permute-start | bytes 6152 | tf_op jit(solution)/shard_map/ppermute | solution.py:14
  18.1 1.3 %collective-permute-start.3 = (f32[1,1,512]{2,1,0:T(1,128)S(1)}, f32[1,1,512]{2,1,0:T(1,128)S(1)}, u32[]{:S(2)}, u32[]{:S(2)}) collective-permute-start(f32[1,1,512]{2,1,0:T(1,128)S(1)} %get-tuple-element.28), channel_id=1, source_target_pairs={{4,0},{8,4},{12,8},{16,12},{20,16},{24,20},{28,24},{5,1},{9,5},{13... | collective-permute-start | bytes 6152 | tf_op jit(solution)/shard_map/ppermute | solution.py:17
  19.4 0.0 collective-permute-done.2
  19.4 4.2 %collective-permute-done.3 = f32[1,1,512]{2,1,0:T(1,128)S(1)} collective-permute-done((f32[1,1,512]{2,1,0:T(1,128)S(1)}, f32[1,1,512]{2,1,0:T(1,128)S(1)}, u32[]{:S(2)}, u32[]{:S(2)}) %collective-permute-start.3) | collective-permute-done | bytes 2080 | tf_op jit(solution)/shard_map/ppermute | solution.py:17
  23.6 0.1 maximum_select_fusion.1
  23.7 0.1 fusion.28
  23.7 0.1 fusion.29
  23.8 0.9 %fusion.16 = f32[1,32,512]{2,1,0:T(8,128)S(1)} fusion(f32[1,32,512]{2,1,0:T(8,128)} %param.6, f32[1,34,512]{2,1,0:T(8,128)S(1)} %maximum_select_fusion.1, f32[1,32,511]{2,1,0:T(8,128)S(1)} %get-tuple-element.13, f32[1,32,1]{2,1,0:T(8,128)S(1)} %get-tuple-element.15, f32[1,32,1]{2,1,0:T(8,128)S(1)} %get-tuple-element.14, f32[1,32,511]{2,1,0:T(8,128)S(1)} %get-tuple-element.12), kind=kLoop, calls=%fused_computation.28 | loop fusion | flops 147456 | bytes 458752 | tf_op jit(solution)/shard_map/add | solution.py:32
  24.8 3.4 %collective-permute-start.4 = (f32[1,1,512]{2,1,0:T(1,128)S(1)}, f32[1,1,512]{2,1,0:T(1,128)S(1)}, u32[]{:S(2)}, u32[]{:S(2)}) collective-permute-start(f32[1,1,512]{2,1,0:T(1,128)S(1)} %get-tuple-element.25), channel_id=1, source_target_pairs={{0,4},{4,8},{8,12},{12,16},{16,20},{20,24},{24,28},{1,5},{5,9},{9,... | collective-permute-start | bytes 6152 | tf_op jit(solution)/shard_map/ppermute | solution.py:14
  28.2 1.3 %collective-permute-start.5 = (f32[1,1,512]{2,1,0:T(1,128)S(1)}, f32[1,1,512]{2,1,0:T(1,128)S(1)}, u32[]{:S(2)}, u32[]{:S(2)}) collective-permute-start(f32[1,1,512]{2,1,0:T(1,128)S(1)} %get-tuple-element.26), channel_id=1, source_target_pairs={{4,0},{8,4},{12,8},{16,12},{20,16},{24,20},{28,24},{5,1},{9,5},{13... | collective-permute-start | bytes 6152 | tf_op jit(solution)/shard_map/ppermute | solution.py:17
  29.5 0.7 compare_select_fusion
  30.2 0.1 reshape.292
  30.3 0.0 collective-permute-done.4
  30.3 3.4 %collective-permute-done.5 = f32[1,1,512]{2,1,0:T(1,128)S(1)} collective-permute-done((f32[1,1,512]{2,1,0:T(1,128)S(1)}, f32[1,1,512]{2,1,0:T(1,128)S(1)}, u32[]{:S(2)}, u32[]{:S(2)}) %collective-permute-start.5) | collective-permute-done | bytes 2080 | tf_op jit(solution)/shard_map/ppermute | solution.py:17
  33.7 0.1 maximum_select_fusion.2
  33.7 0.1 fusion.26
  33.8 0.1 fusion.27
  33.9 0.9 %fusion.11 = f32[1,32,512]{2,1,0:T(8,128)S(1)} fusion(f32[1,32,512]{2,1,0:T(8,128)} %param.6, f32[1,34,512]{2,1,0:T(8,128)S(1)} %maximum_select_fusion.2, f32[1,32,511]{2,1,0:T(8,128)S(1)} %get-tuple-element.9, f32[1,32,1]{2,1,0:T(8,128)S(1)} %get-tuple-element.11, f32[1,32,1]{2,1,0:T(8,128)S(1)} %get-tuple-element.10, f32[1,32,511]{2,1,0:T(8,128)S(1)} %get-tuple-element.8), kind=kLoop, calls=%fused_computation.22 | loop fusion | flops 147456 | bytes 458752 | tf_op jit(solution)/shard_map/add | solution.py:32
  34.8 4.4 %collective-permute-start.6 = (f32[1,1,512]{2,1,0:T(1,128)S(1)}, f32[1,1,512]{2,1,0:T(1,128)S(1)}, u32[]{:S(2)}, u32[]{:S(2)}) collective-permute-start(f32[1,1,512]{2,1,0:T(1,128)S(1)} %get-tuple-element.23), channel_id=1, source_target_pairs={{0,4},{4,8},{8,12},{12,16},{16,20},{20,24},{24,28},{1,5},{5,9},{9,... | collective-permute-start | bytes 6152 | tf_op jit(solution)/shard_map/ppermute | solution.py:14
  39.2 1.3 %collective-permute-start.7 = (f32[1,1,512]{2,1,0:T(1,128)S(1)}, f32[1,1,512]{2,1,0:T(1,128)S(1)}, u32[]{:S(2)}, u32[]{:S(2)}) collective-permute-start(f32[1,1,512]{2,1,0:T(1,128)S(1)} %get-tuple-element.24), channel_id=1, source_target_pairs={{4,0},{8,4},{12,8},{16,12},{20,16},{24,20},{28,24},{5,1},{9,5},{13... | collective-permute-start | bytes 6152 | tf_op jit(solution)/shard_map/ppermute | solution.py:17
  40.5 0.0 collective-permute-done.6
  40.5 4.2 %collective-permute-done.7 = f32[1,1,512]{2,1,0:T(1,128)S(1)} collective-permute-done((f32[1,1,512]{2,1,0:T(1,128)S(1)}, f32[1,1,512]{2,1,0:T(1,128)S(1)}, u32[]{:S(2)}, u32[]{:S(2)}) %collective-permute-start.7) | collective-permute-done | bytes 2080 | tf_op jit(solution)/shard_map/ppermute | solution.py:17
  44.7 0.1 maximum_select_fusion.3
  44.8 0.1 fusion.25
  44.9 0.1 fusion.24
  44.9 1.6 %fusion.22 = (bf16[1,32,512]{2,1,0:T(8,128)(2,1)S(1)}, f32[1,32,512]{2,1,0:T(8,128)}) fusion(f32[1,32,512]{2,1,0:T(8,128)} %param.6, f32[1,32,1]{2,1,0:T(8,128)S(1)} %get-tuple-element.5, f32[1,32,511]{2,1,0:T(8,128)S(1)} %get-tuple-element.7, f32[1,32,511]{2,1,0:T(8,128)S(1)} %get-tuple-element.6, f32[1,32,1]{2,1,0:T(8,128)S(1)} %get-tuple-element.4, ...), kind=kLoop, calls=%fused_computation.49 | loop fusion | flops 163840 | bytes 491520 | tf_op jit(solution)/shard_map/convert_element_type | solution.py:50
  46.5 3.3 %gather_fusion = bf16[1368,128]{1,0:T(8,128)(2,1)S(1)} fusion(bf16[128,128]{1,0:T(8,128)(2,1)S(1)} %convert_element_type.7, s32[2048]{0:T(1024)S(1)} %pad_clamp_fusion), kind=kCustom, calls=%fused_computation | custom fusion | bytes 705888 | tf_op jit(solution)/shard_map/gather | solution.py:51
  49.9 0.8 %reshape.291 = bf16[8,171,128]{2,1,0:T(8,128)(2,1)} reshape(bf16[1368,128]{1,0:T(8,128)(2,1)S(1)} %gather_fusion) | data formatting | bytes 700416 | tf_op jit(solution)/shard_map/gather | solution.py:51
  50.7 3.8 %all-to-all-start = ((bf16[8,171,128]{2,1,0:T(8,128)(2,1)}), bf16[8,171,128]{2,1,0:T(8,128)(2,1)S(1)}, u32[]{:S(2)}, u32[]{:S(2)}) async-start(bf16[8,171,128]{2,1,0:T(8,128)(2,1)} %reshape.291), calls=%async_computation | async-start | bytes 720896 | tf_op jit(solution)/shard_map/all_to_all | solution.py:52
  54.5 0.0 copy-done
  54.5 0.1 copy.10
  54.6 0.1 reshape.300
  54.7 8.7 %all-to-all-done = bf16[8,171,128]{2,1,0:T(8,128)(2,1)S(1)} async-done(((bf16[8,171,128]{2,1,0:T(8,128)(2,1)}), bf16[8,171,128]{2,1,0:T(8,128)(2,1)S(1)}, u32[]{:S(2)}, u32[]{:S(2)}) %all-to-all-start) | async-done | bytes 350240 | tf_op jit(solution)/shard_map/all_to_all | solution.py:52
  63.4 0.1 reshape.288
  63.6 1.9 %gather_fusion.1 = bf16[512,128]{1,0:T(8,128)(2,1)} fusion(bf16[1368,128]{1,0:T(8,128)(2,1)S(1)} %reshape.288, s32[1024]{0:T(1024)S(1)} %pad_clamp_fusion.1), kind=kCustom, calls=%fused_computation.1 | custom fusion | bytes 264192 | tf_op jit(solution)/shard_map/gather | solution.py:54
  65.5 3.3 %all-to-all-start.1 = ((bf16[1,128,4,128]{3,2,0,1:T(4,128)(2,1)}), bf16[1,128,4,128]{3,2,0,1:T(4,128)(2,1)S(1)}, u32[]{:S(2)}, u32[]{:S(2)}) async-start(bf16[1,128,4,128]{3,2,0,1:T(4,128)(2,1)} %bitcast.2), calls=%async_computation.1 | async-start | bytes 262144 | tf_op jit(solution)/shard_map/all_to_all | solution.py:55
  68.8 4.6 %all-to-all-done.1 = bf16[1,128,4,128]{3,2,0,1:T(4,128)(2,1)S(1)} async-done(((bf16[1,128,4,128]{3,2,0,1:T(4,128)(2,1)}), bf16[1,128,4,128]{3,2,0,1:T(4,128)(2,1)S(1)}, u32[]{:S(2)}, u32[]{:S(2)}) %all-to-all-start.1) | async-done | bytes 131104 | tf_op jit(solution)/shard_map/all_to_all | solution.py:55
  73.4 3.4 %convolution_bitcast_fusion = f32[4,32,128]{2,0,1:T(4,128)S(1)} fusion(bf16[32,4,128,128]{3,2,1,0:T(8,128)(2,1)} %param.9, bf16[4,32,4,128]{3,2,1,0:T(4,128)(2,1)S(1)} %bitcast.14), kind=kOutput, calls=%fused_computation.2 | convolution fusion | flops 16777216 | bytes 4390912 | tf_op jit(solution)/shard_map/tkij,ftkj->fti/dot_general | solution.py:56
  76.8 0.1 fusion.1
  76.9 0.1 collective-permute-start.8
  77.0 1.1 %collective-permute-start.9 = (f32[1,32,128]{2,0,1:T(1,128)S(1)}, f32[1,32,128]{2,0,1:T(1,128)S(1)}, u32[]{:S(2)}, u32[]{:S(2)}) collective-permute-start(f32[1,32,128]{2,0,1:T(1,128)S(1)} %get-tuple-element.21), channel_id=1, source_target_pairs={{0,2},{1,3},{2,0},{3,1},{4,6},{5,7},{6,4},{7,5},{8,10},{9,11},{10,... | collective-permute-start | bytes 49160 | tf_op jit(solution)/shard_map/ppermute | solution.py:63
  78.0 0.0 collective-permute-start.10
  78.1 0.3 collective-permute-done.8
  78.4 2.4 %collective-permute-done.9 = f32[1,32,128]{2,0,1:T(1,128)S(1)} collective-permute-done((f32[1,32,128]{2,0,1:T(1,128)S(1)}, f32[1,32,128]{2,0,1:T(1,128)S(1)}, u32[]{:S(2)}, u32[]{:S(2)}) %collective-permute-start.9) | collective-permute-done | bytes 16416 | tf_op jit(solution)/shard_map/ppermute | solution.py:63
  80.8 0.4 collective-permute-done.10
  81.3 0.2 dynamic-slice_reduce_fusion
  81.5 0.6 reshape.289
  (17 shorter events, 0.2 us)
Async XLA Ops:
  1.4 6.2 %collective-permute-start = (f32[1,1,512]{2,1,0:T(1,128)S(1)}, f32[1,1,512]{2,1,0:T(1,128)S(1)}, u32[]{:S(2)}, u32[]{:S(2)}) collective-permute-start(f32[1,1,512]{2,1,0:T(1,128)S(1)} %get-tuple-element.29), channel_id=1, source_target_pairs={{0,4},{4,8},{8,12},{12,16},{16,20},{20,24},{24,28},{1,5},{5,9},{9,... | collective-permute-start | bytes 6152 | tf_op jit(solution)/shard_map/ppermute | solution.py:14
  6.2 5.5 %collective-permute-start.1 = (f32[1,1,512]{2,1,0:T(1,128)S(1)}, f32[1,1,512]{2,1,0:T(1,128)S(1)}, u32[]{:S(2)}, u32[]{:S(2)}) collective-permute-start(f32[1,1,512]{2,1,0:T(1,128)S(1)} %get-tuple-element.30), channel_id=1, source_target_pairs={{4,0},{8,4},{12,8},{16,12},{20,16},{24,20},{28,24},{5,1},{9,5},{13... | collective-permute-start | bytes 6152 | tf_op jit(solution)/shard_map/ppermute | solution.py:17
  12.7 41.8 %copy-start = (s32[128,4]{0,1:T(4,128)S(1)}, s32[128,4]{0,1:T(4,128)}, u32[]{:S(2)}) copy-start(s32[128,4]{0,1:T(4,128)} %param.8) | copy-start | bytes 6148
  13.7 5.7 %collective-permute-start.2 = (f32[1,1,512]{2,1,0:T(1,128)S(1)}, f32[1,1,512]{2,1,0:T(1,128)S(1)}, u32[]{:S(2)}, u32[]{:S(2)}) collective-permute-start(f32[1,1,512]{2,1,0:T(1,128)S(1)} %get-tuple-element.27), channel_id=1, source_target_pairs={{0,4},{4,8},{8,12},{12,16},{16,20},{20,24},{24,28},{1,5},{5,9},{9,... | collective-permute-start | bytes 6152 | tf_op jit(solution)/shard_map/ppermute | solution.py:14
  18.1 5.5 %collective-permute-start.3 = (f32[1,1,512]{2,1,0:T(1,128)S(1)}, f32[1,1,512]{2,1,0:T(1,128)S(1)}, u32[]{:S(2)}, u32[]{:S(2)}) collective-permute-start(f32[1,1,512]{2,1,0:T(1,128)S(1)} %get-tuple-element.28), channel_id=1, source_target_pairs={{4,0},{8,4},{12,8},{16,12},{20,16},{24,20},{28,24},{5,1},{9,5},{13... | collective-permute-start | bytes 6152 | tf_op jit(solution)/shard_map/ppermute | solution.py:17
  24.8 5.5 %collective-permute-start.4 = (f32[1,1,512]{2,1,0:T(1,128)S(1)}, f32[1,1,512]{2,1,0:T(1,128)S(1)}, u32[]{:S(2)}, u32[]{:S(2)}) collective-permute-start(f32[1,1,512]{2,1,0:T(1,128)S(1)} %get-tuple-element.25), channel_id=1, source_target_pairs={{0,4},{4,8},{8,12},{12,16},{16,20},{20,24},{24,28},{1,5},{5,9},{9,... | collective-permute-start | bytes 6152 | tf_op jit(solution)/shard_map/ppermute | solution.py:14
  28.2 5.5 %collective-permute-start.5 = (f32[1,1,512]{2,1,0:T(1,128)S(1)}, f32[1,1,512]{2,1,0:T(1,128)S(1)}, u32[]{:S(2)}, u32[]{:S(2)}) collective-permute-start(f32[1,1,512]{2,1,0:T(1,128)S(1)} %get-tuple-element.26), channel_id=1, source_target_pairs={{4,0},{8,4},{12,8},{16,12},{20,16},{24,20},{28,24},{5,1},{9,5},{13... | collective-permute-start | bytes 6152 | tf_op jit(solution)/shard_map/ppermute | solution.py:17
  34.8 5.7 %collective-permute-start.6 = (f32[1,1,512]{2,1,0:T(1,128)S(1)}, f32[1,1,512]{2,1,0:T(1,128)S(1)}, u32[]{:S(2)}, u32[]{:S(2)}) collective-permute-start(f32[1,1,512]{2,1,0:T(1,128)S(1)} %get-tuple-element.23), channel_id=1, source_target_pairs={{0,4},{4,8},{8,12},{12,16},{16,20},{20,24},{24,28},{1,5},{5,9},{9,... | collective-permute-start | bytes 6152 | tf_op jit(solution)/shard_map/ppermute | solution.py:14
  39.2 5.5 %collective-permute-start.7 = (f32[1,1,512]{2,1,0:T(1,128)S(1)}, f32[1,1,512]{2,1,0:T(1,128)S(1)}, u32[]{:S(2)}, u32[]{:S(2)}) collective-permute-start(f32[1,1,512]{2,1,0:T(1,128)S(1)} %get-tuple-element.24), channel_id=1, source_target_pairs={{4,0},{8,4},{12,8},{16,12},{20,16},{24,20},{28,24},{5,1},{9,5},{13... | collective-permute-start | bytes 6152 | tf_op jit(solution)/shard_map/ppermute | solution.py:17
  50.7 12.7 %all-to-all-start = ((bf16[8,171,128]{2,1,0:T(8,128)(2,1)}), bf16[8,171,128]{2,1,0:T(8,128)(2,1)S(1)}, u32[]{:S(2)}, u32[]{:S(2)}) async-start(bf16[8,171,128]{2,1,0:T(8,128)(2,1)} %reshape.291), calls=%async_computation | async-start | bytes 720896 | tf_op jit(solution)/shard_map/all_to_all | solution.py:52
  65.5 7.9 %all-to-all-start.1 = ((bf16[1,128,4,128]{3,2,0,1:T(4,128)(2,1)}), bf16[1,128,4,128]{3,2,0,1:T(4,128)(2,1)S(1)}, u32[]{:S(2)}, u32[]{:S(2)}) async-start(bf16[1,128,4,128]{3,2,0,1:T(4,128)(2,1)} %bitcast.2), calls=%async_computation.1 | async-start | bytes 262144 | tf_op jit(solution)/shard_map/all_to_all | solution.py:55
  76.9 1.5 %collective-permute-start.8 = (f32[1,32,128]{2,0,1:T(1,128)S(1)}, f32[1,32,128]{2,0,1:T(1,128)S(1)}, u32[]{:S(2)}, u32[]{:S(2)}) collective-permute-start(f32[1,32,128]{2,0,1:T(1,128)S(1)} %get-tuple-element.22), channel_id=1, source_target_pairs={{0,3},{1,0},{2,1},{3,2},{4,7},{5,4},{6,5},{7,6},{8,11},{9,8},{10,9... | collective-permute-start | bytes 49160 | tf_op jit(solution)/shard_map/ppermute | solution.py:63
  77.0 3.8 %collective-permute-start.9 = (f32[1,32,128]{2,0,1:T(1,128)S(1)}, f32[1,32,128]{2,0,1:T(1,128)S(1)}, u32[]{:S(2)}, u32[]{:S(2)}) collective-permute-start(f32[1,32,128]{2,0,1:T(1,128)S(1)} %get-tuple-element.21), channel_id=1, source_target_pairs={{0,2},{1,3},{2,0},{3,1},{4,6},{5,7},{6,4},{7,5},{8,10},{9,11},{10,... | collective-permute-start | bytes 49160 | tf_op jit(solution)/shard_map/ppermute | solution.py:63
  78.0 3.2 %collective-permute-start.10 = (f32[1,32,128]{2,0,1:T(1,128)S(1)}, f32[1,32,128]{2,0,1:T(1,128)S(1)}, u32[]{:S(2)}, u32[]{:S(2)}) collective-permute-start(f32[1,32,128]{2,0,1:T(1,128)S(1)} %get-tuple-element.20), channel_id=1, source_target_pairs={{0,1},{1,2},{2,3},{3,0},{4,5},{5,6},{6,7},{7,4},{8,9},{9,10},{10,1... | collective-permute-start | bytes 49160 | tf_op jit(solution)/shard_map/ppermute | solution.py:63
